TPU v7x, 256 devices: a whole 4x4x8 slice. The times are simulated.
256 devices in a mesh: member: 8 (over x, core), tx: 4 (over y), ty: 8 (over z).
Axes of the slice: x: 4, y: 4, z: 8, core: 2. Of those that a mesh axis runs over, the one named last changes fastest.
Arguments:
- state: float32 [4096, 256, 128], P(('member', 'tx'), 'ty'), parts along dimension 0, may hold values from -6 to 6
- courant: bfloat16 [4096, 256, 128], P(('member', 'tx'), 'ty'), parts along dimension 0, may hold values from -0.3984375 to 0.3984375
- diffusion: float32 [4096, 256], P(('member', 'tx'), 'ty'), parts along dimension 0, may hold values from 0.02 to 0.2
- conv_mask: int32 [4096, 256], P(('member', 'tx'), 'ty'), parts along dimension 0, may hold values from 0 to 1, as said below
- w_in: bfloat16 [128, 1024], replicated, may hold values from -0.5 to 0.5
- w_hidden: bfloat16 [3, 1024, 1024], replicated, may hold values from -0.1875 to 0.1875
- w_out: bfloat16 [1024, 128], replicated, may hold values from -0.1875 to 0.1875
Outputs:
- state_out: float32 [4096, 256, 128], P(('member', 'tx'), 'ty'), parts along dimension 0
There are 8 independent parts, one for each index of `member`. A program takes and returns all parts, laid end to end along the dimension named above; an argument that names none is the same for every part. Nothing has to cross between parts.
Inputs may be any that keep to these rules, and one draw needn't show every extreme that they name: `conv_mask`: A tile is one device's 128 x 32 columns. A tile's used blocks are ceil(its flagged columns / 32); at most 64, reached by some tile; over a member's tiles they sum to exactly 1056.
All inputs are finite; a program needn't handle non-finite values.
Results may differ from a plain program's by a relative error of at most 0.00033.
Values may be sent and summed in bfloat16 or wider, within the bound.
No kernel may reach another device: no remote copies, remote signals or barrier semaphores. Data moves between devices by JAX's collectives and lax.ppermute only.
A program may use at most 64 MiB of HBM per device.

v0:
```python
import jax
import jax.numpy as jnp
from jax import lax
from jax.sharding import PartitionSpec as P

BLK = 32
NBLK = 64
MEAN = 33


def padded_2(value, sides, width):
    for axis, dim in sides:
        count, length = (lax.axis_size(axis), value.shape[dim])
        up = [(i, (i + 1) % count) for i in range(count)]
        down = [(j, i) for i, j in up]
        last = lax.slice_in_dim(value, length - width, length, axis=dim)
        leading = lax.slice_in_dim(value, 0, width, axis=dim)
        before = lax.ppermute(last, axis, up)
        after = lax.ppermute(leading, axis, down)
        value = jnp.concatenate([before, value, after], axis=dim)
    return value


def closure(inputs, w_in, w_hidden, w_out):
    hidden = jax.nn.silu(jnp.dot(inputs, w_in, preferred_element_type=jnp.float32)).astype(
        jnp.bfloat16
    )
    for layer_idx in range(w_hidden.shape[0]):
        hidden = jax.nn.silu(
            jnp.dot(hidden, w_hidden[layer_idx], preferred_element_type=jnp.float32)
        ).astype(jnp.bfloat16)
    return jnp.dot(hidden, w_out, preferred_element_type=jnp.float32).astype(jnp.bfloat16)


def local(state, courant, diffusion, conv_mask, w_in, w_hidden, w_out):
    lon_cells, lat_cells, channels = state.shape
    levels = channels // 2
    padded = padded_2(state, (("tx", 0), ("ty", 1)), 1)
    lat_row = lax.axis_index("ty")
    last_row = lax.axis_size("ty") - 1
    lat_pos = jnp.arange(lat_cells + 2)
    pole_rim = (lat_pos == 0) & (lat_row == 0) | (lat_pos == lat_cells + 1) & (lat_row == last_row)
    padded = jnp.where(pole_rim[None, :, None], jnp.float32(0.0), padded)
    center = padded[1:-1, 1:-1]
    east = padded[2:, 1:-1]
    west = padded[:-2, 1:-1]
    north = padded[1:-1, 2:]
    south = padded[1:-1, :-2]
    wind = courant.astype(jnp.float32)
    along_lon = jnp.concatenate([wind[..., :levels], wind[..., :levels]], -1)
    along_lat = jnp.concatenate([wind[..., levels:], wind[..., levels:]], -1)
    laplace = east + west + north + south - 4.0 * center
    advanced = (
        center
        - 0.5 * along_lon * (east - west)
        - 0.5 * along_lat * (north - south)
        + diffusion[..., None] * laplace
    )
    columns = lon_cells * lat_cells
    capacity = NBLK * BLK
    flags = conv_mask.reshape(columns)
    ranks = jnp.cumsum(flags) - 1
    slot_pos = jnp.where(flags == 1, ranks, capacity)
    features = advanced.reshape(columns, channels).astype(jnp.bfloat16)
    packed = jnp.zeros((capacity, channels), jnp.bfloat16).at[slot_pos].set(features, mode="drop")
    n_tx = lax.axis_size("tx")
    n_ty = lax.axis_size("ty")
    tiles = n_tx * n_ty
    per_pair = NBLK // tiles
    used_blocks = (jnp.sum(flags) + BLK - 1) // BLK
    all_used = lax.all_gather(used_blocks.reshape(1), ("tx", "ty"), axis=0, tiled=True)
    tile_pos = lax.axis_index("tx") * n_ty + lax.axis_index("ty")
    start = jnp.sum(jnp.where(jnp.arange(tiles) < tile_pos, all_used, 0))
    block_ids = jnp.arange(NBLK)
    is_live = block_ids < used_blocks
    targets = (start + block_ids) % tiles
    slot_in = block_ids // tiles
    dest_row = jnp.where(is_live, targets, tiles)
    blocks = packed.reshape(NBLK, BLK, channels)
    outgoing = (
        jnp.zeros((tiles, per_pair, BLK, channels), jnp.bfloat16)
        .at[dest_row, slot_in]
        .set(blocks, mode="drop")
    )
    sent_flags = jnp.zeros((tiles, per_pair), jnp.int32).at[dest_row, slot_in].set(1, mode="drop")
    arrived, arrived_flags = (
        lax.all_to_all(outgoing, ("tx", "ty"), split_axis=0, concat_axis=0, tiled=True),
        lax.all_to_all(sent_flags, ("tx", "ty"), split_axis=0, concat_axis=0, tiled=True),
    )
    order = jnp.argsort(1 - arrived_flags.reshape(tiles * per_pair), stable=True)[:MEAN]
    chosen = arrived.reshape(tiles * per_pair, BLK, channels)[order]
    results = closure(chosen.reshape(MEAN * BLK, channels), w_in, w_hidden, w_out)
    returning = (
        jnp.zeros((tiles * per_pair, BLK, channels), jnp.bfloat16)
        .at[order]
        .set(results.reshape(MEAN, BLK, channels))
    )
    returned = lax.all_to_all(
        returning.reshape(tiles, per_pair, BLK, channels),
        ("tx", "ty"),
        split_axis=0,
        concat_axis=0,
        tiled=True,
    )
    mine = returned[jnp.where(is_live, targets, 0), slot_in]
    packed_tend = mine.reshape(capacity, channels)
    picked = packed_tend[jnp.minimum(slot_pos, capacity - 1)].astype(jnp.float32)
    added = jnp.where(flags[:, None] == 1, picked, jnp.float32(0.0))
    return (advanced.reshape(columns, channels) + added).reshape(lon_cells, lat_cells, channels)


def solution(mesh):
    return jax.shard_map(
        local,
        mesh=mesh,
        in_specs=(
            P(("member", "tx"), "ty", None),
            P(("member", "tx"), "ty", None),
            P(("member", "tx"), "ty"),
            P(("member", "tx"), "ty"),
            P(),
            P(),
            P(),
        ),
        out_specs=P(("member", "tx"), "ty", None),
        check_vma=False,
    )
```

profile of v0, /device:TPU:34, one launch (start us, length us, event | category | flops | bytes accessed | tf_op | source)
XLA Modules:
  0.0 163.4 jit_solution(3328563770658946981)
XLA Ops:
  0.0 0.8 fusion.38
  0.8 1.6 collective-permute-start
  2.4 1.7 %collective-permute-start.1 = (f32[1,32,128]{2,1,0:T(8,128)S(1)}, f32[1,32,128]{2,1,0:T(8,128)S(1)}, u32[]{:S(2)}, u32[]{:S(2)}) collective-permute-start(f32[1,32,128]{2,1,0:T(8,128)S(1)} %get-tuple-element.11), channel_id=1, source_target_pairs={{8,0},{16,8},{24,16},{0,24},{9,1},{17,9},{25,17},{1,25},{10,2},{18... | collective-permute-start | bytes 49160 | tf_op jit(solution)/shard_map/ppermute | solution.py:19
  4.1 1.4 reduce_sum.18
  6.1 1.3 dynamic-slice
  7.4 0.8 dynamic-update-slice
  8.1 21.7 %all-reduce = s32[32]{0:T(128)S(1)} all-reduce(s32[32]{0:T(128)S(1)} %dynamic-update-slice), channel_id=1, replica_groups=mesh['member'=8,'tx'=4,'ty'=8] {'tx','ty'}, use_global_device_ids=true, to_apply=%add | all-reduce | flops 32 | bytes 256
  29.8 0.6 fusion.26
  30.5 0.6 fusion.32
  31.1 3.5 %scatter_fusion = s32[32,2]{0,1:T(2,128)S(1)} fusion(s32[32,2]{0,1:T(2,128)S(1)} %broadcast_in_dim.65, s32[64]{0:T(128)S(1)} %fusion.32, s32[64]{0:T(128)S(1)} %broadcast.374), kind=kCustom, calls=%fused_computation.3 | custom fusion | bytes 1280 | tf_op jit(solution)/shard_map/scatter | solution.py:85
  34.6 0.7 copy.31
  35.3 5.2 %all-to-all-start = ((s32[32,1,2]{2,1,0:T(1,128)}), s32[32,1,2]{2,1,0:T(1,128)S(1)}, u32[]{:S(2)}, u32[]{:S(2)}) async-start(s32[32,1,2]{2,1,0:T(1,128)} %copy.31), calls=%async_computation | async-start | bytes 32768 | tf_op jit(solution)/shard_map/all_to_all | solution.py:88
  40.6 0.7 broadcast_compare_fusion
  41.3 0.8 copy.33
  42.1 0.1 copy.30
  42.2 0.1 eq.61
  42.4 0.3 reduce-window.9
  42.8 0.1 slice_reduce_fusion
  43.0 0.7 compare_select_fusion
  43.7 2.5 %fusion.39 = (f32[128,32,64]{2,1,0:T(8,128)}, f32[128,32,64]{2,1,0:T(8,128)}) fusion(bf16[128,32,128]{2,1,0:T(8,128)(2,1)S(1)} %copy-done.1), kind=kLoop, calls=%fused_computation.76 | loop fusion | bytes 4194304 | tf_op jit(solution)/shard_map/slice | solution.py:50
  46.4 0.2 constant_dynamic-update-slice_fusion.1
  46.7 0.3 collective-permute-start.3
  47.0 1.8 %collective-permute-start.2 = (f32[130,1,128]{2,0,1:T(8,128)S(1)}, f32[130,1,128]{2,0,1:T(8,128)S(1)}, u32[]{:S(2)}, u32[]{:S(2)}) collective-permute-start(f32[130,1,128]{2,0,1:T(8,128)S(1)} %copy.25), channel_id=1, source_target_pairs={{0,1},{1,2},{2,3},{3,4},{4,5},{5,6},{6,7},{7,0},{8,9},{9,10},{10,1... | collective-permute-start | bytes 199688 | tf_op jit(solution)/shard_map/ppermute | solution.py:18
  48.8 2.3 %collective-permute-done.3 = f32[130,1,128]{2,0,1:T(8,128)S(1)} collective-permute-done((f32[130,1,128]{2,0,1:T(8,128)S(1)}, f32[130,1,128]{2,0,1:T(8,128)S(1)}, u32[]{:S(2)}, u32[]{:S(2)}) %collective-permute-start.3) | collective-permute-done | bytes 66592 | tf_op jit(solution)/shard_map/ppermute | solution.py:19
  51.2 1.1 collective-permute-done.2
  52.4 0.5 maximum_select_fusion
  52.9 1.1 copy-done.2
  54.0 0.6 copy-done.3
  54.6 3.4 %fusion.35 = (bf16[128,32,128]{2,1,0:T(8,128)(2,1)}, f32[128,32,128]{2,1,0:T(8,128)S(1)}) fusion(f32[128,32]{1,0:T(8,128)S(1)} %copy.29, f32[130,34,128]{2,1,0:T(8,128)S(1)} %maximum_select_fusion, f32[128,32,64]{2,1,0:T(8,128)S(1)} %copy-done.3, f32[128,32,64]{2,1,0:T(8,128)S(1)} %copy-done.2), kind=kLoop, calls=%fused_computation.73 | loop fusion | flops 9437184 | bytes 15745024 | tf_op jit(solution)/shard_map/convert_element_type | solution.py:64
  58.1 11.2 %scatter_custom_fusion.1 = bf16[2048,128]{1,0:T(8,128)(2,1)S(1)} fusion(s32[4096]{0:T(1024)} %bitcast.51, bf16[4096,128]{1,0:T(8,128)(2,1)} %bitcast.46, bf16[]{:T(256)} %constant.83.clone.1), kind=kCustom, calls=%fused_computation.31 | custom fusion | bytes 524800 | tf_op jit(solution)/shard_map/scatter | solution.py:65
  69.3 0.9 broadcast_in_dim.68
  70.2 7.0 %scatter_fusion.1 = bf16[32,2,32,128]{3,2,1,0:T(8,128)(2,1)} fusion(bf16[32,2,32,128]{3,2,1,0:T(8,128)(2,1)} %broadcast_in_dim.68, s32[64]{0:T(128)S(1)} %fusion.32, bf16[64,32,128]{2,1,0:T(8,128)(2,1)S(1)} %bitcast.44), kind=kCustom, calls=%fused_computation.5 | custom fusion | bytes 1573376 | tf_op jit(solution)/shard_map/scatter | solution.py:83
  77.3 10.6 %all-to-all-start.1 = ((bf16[32,2,32,128]{3,2,1,0:T(8,128)(2,1)}), bf16[32,2,32,128]{3,2,1,0:T(8,128)(2,1)S(1)}, u32[]{:S(2)}, u32[]{:S(2)}) async-start(bf16[32,2,32,128]{3,2,1,0:T(8,128)(2,1)} %scatter_fusion.1), calls=%async_computation.1 | async-start | bytes 1048576 | tf_op jit(solution)/shard_map/all_to_all | solution.py:87
  87.9 0.1 sub.50
  88.0 2.1 %sort.17 = (s32[64]{0:T(128)}, s32[64]{0:T(128)S(1)}) sort(s32[64]{0:T(128)S(1)} %sub.50, s32[64]{0:T(128)S(1)} %iota.32), dimensions={0}, to_apply=%region_3.4 | sort | flops 384 | bytes 1024 | tf_op jit(solution)/shard_map/jit(argsort)/sort | solution.py:90
  90.2 11.1 %all-to-all-done.1 = bf16[32,2,32,128]{3,2,1,0:T(8,128)(2,1)S(1)} async-done(((bf16[32,2,32,128]{3,2,1,0:T(8,128)(2,1)}), bf16[32,2,32,128]{3,2,1,0:T(8,128)(2,1)S(1)}, u32[]{:S(2)}, u32[]{:S(2)}) %all-to-all-start.1) | async-done | bytes 524320 | tf_op jit(solution)/shard_map/all_to_all | solution.py:87
  101.3 0.6 gather_fusion
  101.9 2.7 %multiply_convert_fusion.3 = bf16[1056,1024]{1,0:T(8,128)(2,1)} fusion(bf16[1056,128]{1,0:T(8,128)(2,1)S(1)} %bitcast.47, bf16[128,1024]{1,0:T(8,128)(2,1)S(1)} %copy-done), kind=kOutput, calls=%fused_computation.10 | convolution fusion | flops 282230784 | bytes 2695168 | tf_op jit(solution)/shard_map/dot_general | solution.py:25
  104.6 9.5 %multiply_convert_fusion.1 = bf16[1056,1024]{1,0:T(8,128)(2,1)} fusion(bf16[3,1024,1024]{2,1,0:T(8,128)(2,1)} %param.12, bf16[1056,1024]{1,0:T(8,128)(2,1)} %multiply_convert_fusion.3), kind=kOutput, calls=%fused_computation.8 | convolution fusion | flops 4439998464 | bytes 8519680 | tf_op jit(solution)/shard_map/dot_general | solution.py:30
  114.1 5.4 %convolution_convert_fusion = bf16[1056,128]{1,0:T(8,128)(2,1)S(1)} fusion(bf16[1024,128]{1,0:T(8,128)(2,1)S(1)} %copy-done.6, bf16[1056,1024]{1,0:T(8,128)(2,1)} %multiply_convert_fusion.1, bf16[3,1024,1024]{2,1,0:T(8,128)(2,1)} %param.12), kind=kOutput, calls=%fused_computation.12 | convolution fusion | flops 2496958464 | bytes 4792320 | tf_op jit(solution)/shard_map/dot_general | solution.py:32
  119.5 0.9 broadcast_in_dim.64
  120.3 5.3 %scatter_fusion.2 = bf16[64,32,128]{2,1,0:T(8,128)(2,1)} fusion(bf16[64,32,128]{2,1,0:T(8,128)(2,1)} %broadcast_in_dim.64, s32[33]{0:T(128)S(1)} %compare_select_fusion.3, bf16[33,32,128]{2,1,0:T(8,128)(2,1)S(1)} %bitcast.48), kind=kCustom, calls=%fused_computation.6 | custom fusion | bytes 811140 | tf_op jit(solution)/shard_map/scatter | solution.py:96
  125.6 4.9 %all-to-all-start.2 = ((bf16[32,2,32,128]{3,2,1,0:T(8,128)(2,1)}), bf16[32,2,32,128]{3,2,1,0:T(8,128)(2,1)S(1)}, u32[]{:S(2)}, u32[]{:S(2)}) async-start(bf16[32,2,32,128]{3,2,1,0:T(8,128)(2,1)} %bitcast.14), calls=%async_computation.2 | async-start | bytes 1048576 | tf_op jit(solution)/shard_map/all_to_all | solution.py:98
  130.5 0.6 fusion.31
  131.2 12.8 %all-to-all-done.2 = bf16[32,2,32,128]{3,2,1,0:T(8,128)(2,1)S(1)} async-done(((bf16[32,2,32,128]{3,2,1,0:T(8,128)(2,1)}), bf16[32,2,32,128]{3,2,1,0:T(8,128)(2,1)S(1)}, u32[]{:S(2)}, u32[]{:S(2)}) %all-to-all-start.2) | async-done | bytes 524320 | tf_op jit(solution)/shard_map/all_to_all | solution.py:98
  143.9 0.7 gather_fusion.1
  144.7 14.9 %gather_fusion.2 = bf16[4096,128]{1,0:T(8,128)(2,1)} fusion(bf16[2048,128]{1,0:T(8,128)(2,1)S(1)} %bitcast.42, s32[4096]{0:T(1024)S(1)} %broadcast_clamp_fusion), kind=kCustom, calls=%fused_computation.2 | custom fusion | bytes 2113536 | tf_op jit(solution)/shard_map/gather | solution.py:107
  159.6 3.8 %fusion.6 = f32[128,32,128]{2,1,0:T(8,128)} fusion(f32[128,32,128]{2,1,0:T(8,128)S(1)} %get-tuple-element.8, bf16[128,32,128]{2,1,0:T(8,128)(2,1)} %bitcast.43, pred[128,32]{1,0:T(8,128)(4,1)S(1)} %copy.30), kind=kLoop, calls=%fused_computation.22 | loop fusion | flops 1572864 | bytes 5246976 | tf_op jit(solution)/shard_map/add | solution.py:109
  (36 shorter events, 0.7 us)
Async XLA Ops:
  0.0 101.9 %copy-start = (bf16[128,1024]{1,0:T(8,128)(2,1)S(1)}, bf16[128,1024]{1,0:T(8,128)(2,1)}, u32[]{:S(2)}) copy-start(bf16[128,1024]{1,0:T(8,128)(2,1)} %param.11) | copy-start | bytes 786436
  0.0 43.7 %copy-start.1 = (bf16[128,32,128]{2,1,0:T(8,128)(2,1)S(1)}, bf16[128,32,128]{2,1,0:T(8,128)(2,1)}, u32[]{:S(2)}) copy-start(bf16[128,32,128]{2,1,0:T(8,128)(2,1)} %param.8) | copy-start | bytes 3145732
  0.8 45.5 %collective-permute-start = (f32[1,32,128]{2,1,0:T(8,128)S(1)}, f32[1,32,128]{2,1,0:T(8,128)S(1)}, u32[]{:S(2)}, u32[]{:S(2)}) collective-permute-start(f32[1,32,128]{2,1,0:T(8,128)S(1)} %get-tuple-element.12), channel_id=1, source_target_pairs={{0,8},{8,16},{16,24},{24,0},{1,9},{9,17},{17,25},{25,1},{2,10},{10... | collective-permute-start | bytes 49160 | tf_op jit(solution)/shard_map/ppermute | solution.py:18
  2.4 44.1 %collective-permute-start.1 = (f32[1,32,128]{2,1,0:T(8,128)S(1)}, f32[1,32,128]{2,1,0:T(8,128)S(1)}, u32[]{:S(2)}, u32[]{:S(2)}) collective-permute-start(f32[1,32,128]{2,1,0:T(8,128)S(1)} %get-tuple-element.11), channel_id=1, source_target_pairs={{8,0},{16,8},{24,16},{0,24},{9,1},{17,9},{25,17},{1,25},{10,2},{18... | collective-permute-start | bytes 49160 | tf_op jit(solution)/shard_map/ppermute | solution.py:19
  35.3 41.9 %all-to-all-start = ((s32[32,1,2]{2,1,0:T(1,128)}), s32[32,1,2]{2,1,0:T(1,128)S(1)}, u32[]{:S(2)}, u32[]{:S(2)}) async-start(s32[32,1,2]{2,1,0:T(1,128)} %copy.31), calls=%async_computation | async-start | bytes 32768 | tf_op jit(solution)/shard_map/all_to_all | solution.py:88
  43.7 2.6 %copy-start.5 = (f32[128,32]{0,1:T(8,128)S(1)}, f32[128,32]{0,1:T(8,128)}, u32[]{:S(2)}) copy-start(f32[128,32]{0,1:T(8,128)} %param.9) | copy-start | bytes 49156
  43.7 2.7 %copy-start.4 = (f32[128,32,128]{2,1,0:T(8,128)S(1)}, f32[128,32,128]{2,1,0:T(8,128)}, u32[]{:S(2)}) copy-start(f32[128,32,128]{2,1,0:T(8,128)} %param.7) | copy-start | bytes 6291460
  46.7 4.4 %collective-permute-start.3 = (f32[130,1,128]{2,0,1:T(8,128)S(1)}, f32[130,1,128]{2,0,1:T(8,128)S(1)}, u32[]{:S(2)}, u32[]{:S(2)}) collective-permute-start(f32[130,1,128]{2,0,1:T(8,128)S(1)} %copy.26), channel_id=1, source_target_pairs={{1,0},{2,1},{3,2},{4,3},{5,4},{6,5},{7,6},{0,7},{9,8},{10,9},{11,1... | collective-permute-start | bytes 199688 | tf_op jit(solution)/shard_map/ppermute | solution.py:19
  47.0 5.3 %collective-permute-start.2 = (f32[130,1,128]{2,0,1:T(8,128)S(1)}, f32[130,1,128]{2,0,1:T(8,128)S(1)}, u32[]{:S(2)}, u32[]{:S(2)}) collective-permute-start(f32[130,1,128]{2,0,1:T(8,128)S(1)} %copy.25), channel_id=1, source_target_pairs={{0,1},{1,2},{2,3},{3,4},{4,5},{5,6},{6,7},{7,0},{8,9},{9,10},{10,1... | collective-permute-start | bytes 199688 | tf_op jit(solution)/shard_map/ppermute | solution.py:18
  52.4 1.6 copy-start.2
  52.4 2.2 %copy-start.3 = (f32[128,32,64]{2,1,0:T(8,128)S(1)}, f32[128,32,64]{2,1,0:T(8,128)}, u32[]{:S(2)}) copy-start(f32[128,32,64]{2,1,0:T(8,128)} %get-tuple-element.14) | copy-start | bytes 3145732
  77.3 24.0 %all-to-all-start.1 = ((bf16[32,2,32,128]{3,2,1,0:T(8,128)(2,1)}), bf16[32,2,32,128]{3,2,1,0:T(8,128)(2,1)S(1)}, u32[]{:S(2)}, u32[]{:S(2)}) async-start(bf16[32,2,32,128]{3,2,1,0:T(8,128)(2,1)} %scatter_fusion.1), calls=%async_computation.1 | async-start | bytes 1048576 | tf_op jit(solution)/shard_map/all_to_all | solution.py:87
  104.6 9.5 %copy-start.6 = (bf16[1024,128]{1,0:T(8,128)(2,1)S(1)}, bf16[1024,128]{1,0:T(8,128)(2,1)}, u32[]{:S(2)}) copy-start(bf16[1024,128]{1,0:T(8,128)(2,1)} %param.13) | copy-start | bytes 786436
  125.6 18.3 %all-to-all-start.2 = ((bf16[32,2,32,128]{3,2,1,0:T(8,128)(2,1)}), bf16[32,2,32,128]{3,2,1,0:T(8,128)(2,1)S(1)}, u32[]{:S(2)}, u32[]{:S(2)}) async-start(bf16[32,2,32,128]{3,2,1,0:T(8,128)(2,1)} %bitcast.14), calls=%async_computation.2 | async-start | bytes 1048576 | tf_op jit(solution)/shard_map/all_to_all | solution.py:98
where the time goes:
time: 165 us; the launch traced here: 163 us
  local copies, waits for them, and re-layouts  54.9 us (33%)
  waiting for transfers between devices  27.3 us (17%)
  starting transfers between devices  26 us (16%)
  blocking collectives  21.7 us (13%)
  matrix products  17.6 us (11%)
  other arithmetic  14.9 us (9%)
    unnamed x1, blocking collectives  21.7 us
    gather x1, local copies, waits for them, and re-layouts, local(): packed_tend[jnp.minimum(slot_pos, capacity - 1)].astype(jnp.float32)  14.9 us
    all_to_all x1, waiting for transfers between devices, local(): lax.all_to_all(returning.reshape(tiles, per_pair, BLK, channels), ('tx',...  12.8 us
    scatter x1, local copies, waits for them, and re-layouts, local(): jnp.zeros((capacity, channels), jnp.bfloat16).at[slot_pos]  11.2 us
    all_to_all x1, waiting for transfers between devices, local(): lax.all_to_all(outgoing, ('tx', 'ty'), split_axis=0, concat_axis=0, tiled...  11.1 us
    all_to_all x1, starting transfers between devices, local(): lax.all_to_all(outgoing, ('tx', 'ty'), split_axis=0, concat_axis=0, tiled...  10.6 us
    dot_general x1, matrix products, closure(): jnp.dot(hidden, w_hidden[layer_idx], preferred_element_type=jnp.float32)  9.51 us
    scatter x1, local copies, waits for them, and re-layouts, local(): outgoing = jnp.zeros((tiles, per_pair, BLK, channels), jnp.bfloat16).at[d...  7.03 us
  transfers between devices with their start and end apart: 7, of which 4 were waited for; matrix products, arithmetic and copies ran while one was open for 25% of the time, Pallas kernels for 0%

commit v1 on v0

v1 whole, which is shorter than its diff:
```python
import functools

import jax
import jax.numpy as jnp
from jax import lax
from jax.experimental import pallas as pl
from jax.experimental.pallas import tpu as pltpu
from jax.sharding import PartitionSpec as P

LON, LAT, CH, HID = 128, 32, 128, 1024
COLS = LON * LAT
TILE = 512
CAP = 2048
ROWS = CAP + TILE
PGRP = 256
UGRP = 128
EDGE = 384
BF, F32, I32 = jnp.bfloat16, jnp.float32, jnp.int32


def iota(shape, dim):
    return lax.broadcasted_iota(I32, shape, dim)


def one_hot(hit):
    return jnp.where(hit, F32(1.0), F32(0.0)).astype(BF)


def mm(a, b):
    return jnp.dot(a, b, preferred_element_type=F32)


def silu(v):
    half = 0.5 * v
    return (half + half * jnp.tanh(half)).astype(BF)


def closure_tile(x, w_in, w_hid, w_out, ha, hb):
    step = 256

    def layer(src, weight, dst):
        for n in range(0, HID, step):
            dst[:, n : n + step] = silu(mm(src, weight(n)))

    layer(x, lambda n: w_in[:, n : n + step], ha)
    layer(ha[...], lambda n: w_hid[0, :, n : n + step], hb)
    layer(hb[...], lambda n: w_hid[1, :, n : n + step], ha)
    layer(ha[...], lambda n: w_hid[2, :, n : n + step], hb)
    return mm(hb[...], w_out[...]).astype(BF)


def append(packed, hits, features, aligned):
    rows = mm(one_hot(hits), features)
    n = rows.shape[0]
    head = packed[pl.ds(aligned, 16), :].astype(F32) + rows[:16]
    packed[pl.ds(aligned, 16), :] = head.astype(BF)
    packed[pl.ds(pl.multiple_of(aligned + 16, 16), n - 16), :] = rows[16:].astype(BF)


def align16(x):
    return pl.multiple_of((x // 16) * 16, 16)


def first_kernel(
    state_h, courant_h, diff_h, mask_h, win_h, whid_h, wout_h,
    adv, packed, tend, rank_t, rank_e, scal, coef, w_in, w_hid, w_out,
    st, cou, dif, msk, dif_t, rank_n, rank_r, tmp, ha, hb, scal_s, sem, sem_s,
):
    quarter = COLS // 4

    def in_copies(k):
        return (
            pltpu.make_async_copy(state_h.at[pl.ds(k * quarter, quarter)], st.at[pl.ds(k * quarter + LAT, quarter)], sem.at[k]),
            pltpu.make_async_copy(courant_h.at[pl.ds(k * quarter, quarter)], cou.at[pl.ds(k * quarter, quarter)], sem.at[4 + k]),
        )

    mask_copy = pltpu.make_async_copy(mask_h, msk, sem.at[8])
    diff_copy = pltpu.make_async_copy(diff_h, dif, sem.at[9])
    w_copies = (
        pltpu.make_async_copy(win_h, w_in, sem.at[10]),
        pltpu.make_async_copy(whid_h, w_hid, sem.at[11]),
        pltpu.make_async_copy(wout_h, w_out, sem.at[12]),
    )
    mask_copy.start()
    diff_copy.start()
    for k in range(4):
        for c in in_copies(k):
            c.start()
    for c in w_copies:
        c.start()
    packed[...] = jnp.zeros_like(packed)
    tend[...] = jnp.zeros_like(tend)
    st[0:LAT, :] = jnp.zeros((LAT, CH), F32)
    st[COLS + LAT : COLS + 2 * LAT, :] = jnp.zeros((LAT, CH), F32)

    mask_copy.wait()
    lon, lat = iota((LON, LAT), 0), iota((LON, LAT), 1)
    flags = msk[...]
    inner = (lon > 0) & (lon < LON - 1) & (lat > 0) & (lat < LAT - 1) & (flags == 1)
    inner_b = one_hot(inner)
    before = one_hot(iota((LAT, LAT), 0) < iota((LAT, LAT), 1))
    in_row = mm(inner_b, before)
    rows_below = one_hot(iota((LON, LON), 1) < iota((LON, LON), 0))
    per_lat = mm(rows_below, inner_b).astype(BF)
    row_start = mm(per_lat, jnp.ones((LAT, LON), BF))
    rank = jnp.where(inner, in_row + row_start[:, :LAT], F32(-4096.0))
    wide = jnp.concatenate([rank, jnp.zeros((LON, LON - LAT), F32)], axis=1)
    rank_n[...] = wide
    rank_t[...] = jnp.transpose(wide)[:LAT].astype(I32)
    rank_r[...] = jnp.concatenate(
        [rank_n[pl.ds(j, COLS // PGRP, stride=PGRP // LAT), :LAT] for j in range(PGRP // LAT)], axis=1
    ).astype(I32)
    starts = jnp.transpose(row_start)[:1]

    flags_f = flags.astype(F32)
    flags_w = jnp.concatenate([flags_f, jnp.zeros((LON, LON - LAT), F32)], axis=1)
    flags_t = jnp.transpose(flags_w)
    lane = iota((1, LON), 1)
    ends = (lane == 0) | (lane == LON - 1)
    edge_row = jnp.concatenate(
        [
            flags_f[:1],
            flags_f[LON - 1 :],
            jnp.zeros((1, 64), F32),
            jnp.where(ends, F32(0.0), flags_t[:1]),
            jnp.where(ends, F32(0.0), flags_t[LAT - 1 : LAT]),
        ],
        axis=1,
    )
    edge_b = jnp.broadcast_to(edge_row, (16, EDGE)).astype(BF)
    edge_before = one_hot(iota((EDGE, EDGE), 0) < iota((EDGE, EDGE), 1))
    edge_rank = mm(edge_b, edge_before)[:8]
    inner_n = starts[:, LON - 1 :]
    rank_e[...] = jnp.where(edge_row == 1.0, edge_rank + inner_n, F32(-4096.0)).astype(I32)
    edge_n = jnp.broadcast_to(jnp.sum(edge_row, axis=1, keepdims=True), (1, LON))
    rows8 = iota((8, LON), 0)
    scal[...] = jnp.where(rows8 == 0, starts, edge_n).astype(I32)
    scal_copy = pltpu.make_async_copy(scal, scal_s, sem_s)
    scal_copy.start()
    diff_copy.wait()
    dif_w = jnp.concatenate([dif[...], jnp.zeros((LON, LON - LAT), F32)], axis=1)
    dif_t[...] = jnp.transpose(dif_w)[:LAT]
    scal_copy.wait()

    for c in in_copies(0):
        c.wait()

    def group(g, carry):
        k = lax.div(g, 4)

        @pl.when((lax.rem(g, 4) == 3) & (g < 15))
        def _():
            for c in in_copies(k + 1):
                c.wait()

        r = pl.multiple_of(g * PGRP, PGRP)
        center = st[pl.ds(r + LAT, PGRP), :]
        east = st[pl.ds(r + 2 * LAT, PGRP), :]
        west = st[pl.ds(r, PGRP), :]
        row = iota((PGRP, CH), 0)
        lat_of = lax.rem(row, LAT)
        north = jnp.where(lat_of == LAT - 1, F32(0.0), st[pl.ds(r + LAT + 1, PGRP), :])
        south = jnp.where(lat_of == 0, F32(0.0), st[pl.ds(r + LAT - 1, PGRP), :])
        wind = 0.5 * cou[pl.ds(r, PGRP), :].astype(F32)
        turned = pltpu.roll(wind, 64, 1)
        low = iota((PGRP, CH), 1) < 64
        along_lon = jnp.where(low, wind, turned)
        along_lat = jnp.where(low, turned, wind)
        d8 = pltpu.roll(dif_t[...], lax.rem(LON - g * 8, LON), 1)
        d = jnp.concatenate([jnp.broadcast_to(d8[:, j : j + 1], (LAT, CH)) for j in range(8)], axis=0)
        laplace = east + west + north + south - 4.0 * center
        new = center - along_lon * (east - west) - along_lat * (north - south) + d * laplace
        adv[pl.ds(r, PGRP), :] = new
        tmp[...] = d - along_lat
        coef[pl.ds(pl.multiple_of(g * 8, 8), 8), :] = tmp[pl.ds(LAT - 1, 8, stride=LAT), :]
        tmp[...] = d + along_lat
        coef[pl.ds(pl.multiple_of(LON + g * 8, 8), 8), :] = tmp[pl.ds(0, 8, stride=LAT), :]

        @pl.when(g == 0)
        def _():
            coef[2 * LON : 2 * LON + LAT, :] = (d + along_lon)[:LAT]

        @pl.when(g == 15)
        def _():
            coef[2 * LON + LAT : 2 * LON + 2 * LAT, :] = (d - along_lon)[PGRP - LAT :]

        aligned = align16(scal_s[0, g * 8])
        hits = iota((PGRP + 16, PGRP), 0) == rank_r[pl.ds(g, 1), :] - aligned
        append(packed, hits, new.astype(BF), aligned)
        return carry

    lax.fori_loop(0, 16, group, 0)
    for c in w_copies:
        c.wait()

    @pl.when(scal_s[0, LON - 1] >= TILE)
    def _():
        tend[:TILE, :] = closure_tile(packed[:TILE, :], w_in, w_hid, w_out, ha, hb)


def second_kernel(
    west, east, south, north, adv_i, packed_i, tend_i, rank_t, rank_e, scal, coef, w_in, w_hid, w_out,
    out_h, adv, packed, tend, ha, hb, scal_s, sem_s, sem,
):
    scal_copy = pltpu.make_async_copy(scal, scal_s, sem_s)
    scal_copy.start()
    adv[...] = adv_i[...]
    packed[...] = packed_i[...]
    tend[...] = tend_i[...]
    adv[0:LAT, :] += west[...] * coef[2 * LON : 2 * LON + LAT, :]
    adv[COLS - LAT :, :] += east[...] * coef[2 * LON + LAT :, :]
    low, high = pl.ds(0, LON, stride=LAT), pl.ds(LAT - 1, LON, stride=LAT)
    adv[high, :] = adv[high, :] + north[...] * coef[:LON, :]
    adv[low, :] = adv[low, :] + south[...] * coef[LON : 2 * LON, :]
    edge = jnp.concatenate(
        [adv[0:LAT, :], adv[COLS - LAT :, :], jnp.zeros((64, CH), F32), adv[low, :], adv[high, :]], axis=0
    ).astype(BF)
    scal_copy.wait()
    inner_n = scal_s[0, LON - 1]
    count = inner_n + scal_s[1, 0]
    aligned_e = align16(inner_n)
    hits = iota((320 + 16, EDGE), 0) == rank_e[:1, :] - aligned_e
    append(packed, hits, edge, aligned_e)

    def tile(t, carry):
        r = pl.multiple_of(t * TILE, TILE)
        tend[pl.ds(r, TILE), :] = closure_tile(packed[pl.ds(r, TILE), :], w_in, w_hid, w_out, ha, hb)
        return carry

    done = jnp.where(inner_n >= TILE, 1, 0)
    lax.fori_loop(done, lax.div(count + TILE - 1, TILE), tile, 0)

    rank_col = jnp.concatenate(
        [jnp.transpose(jnp.broadcast_to(rank_e[:1, k * 128 : k * 128 + 128], (128, 128))) for k in range(3)], axis=0
    )
    picks = jnp.concatenate([rank_col - aligned_e - 128 * k for k in range(3)], axis=1) == lax.rem(
        iota((EDGE, EDGE), 1), 128
    )
    back = mm(one_hot(picks), tend[pl.ds(aligned_e, EDGE), :])
    adv[0:LAT, :] += back[0:LAT]
    adv[COLS - LAT :, :] += back[LAT : 2 * LAT]
    adv[low, :] = adv[low, :] + back[128:256]
    adv[high, :] = adv[high, :] + back[256:384]

    def out_copy(k):
        part = pl.ds(k * (COLS // 8), COLS // 8)
        return pltpu.make_async_copy(adv.at[part], out_h.at[part], sem.at[k])

    def unpack(g, carry):
        r = pl.multiple_of(g * UGRP, UGRP)
        aligned = align16(scal_s[0, g * 4])
        local = rank_t[...] - aligned
        local = pltpu.roll(local, lax.rem(LON - g * 4, LON), 1)
        col = jnp.concatenate([jnp.broadcast_to(local[:, j : j + 1], (LAT, 256)) for j in range(4)], axis=0)
        hit = one_hot(col == iota((UGRP, 256), 1))
        adv[pl.ds(r, UGRP), :] += mm(hit, tend[pl.ds(aligned, 256), :])

        @pl.when(lax.rem(g, 4) == 3)
        def _():
            out_copy(lax.div(g, 4)).start()

        return carry

    lax.fori_loop(0, COLS // UGRP, unpack, 0)
    for k in range(8):
        out_copy(k).wait()


ANY = pl.BlockSpec(memory_space=pl.ANY)
VM = pl.BlockSpec(memory_space=pltpu.VMEM)


def local(state, courant, diffusion, conv_mask, w_in, w_hidden, w_out):
    n_tx, n_ty = lax.axis_size("tx"), lax.axis_size("ty")
    ring = [(i, (i + 1) % n_tx) for i in range(n_tx)]
    line = [(i, i + 1) for i in range(n_ty - 1)]
    west = lax.ppermute(state[LON - 1], "tx", ring)
    east = lax.ppermute(state[0], "tx", [(j, i) for i, j in ring])
    south = lax.ppermute(state[:, LAT - 1], "ty", line)
    north = lax.ppermute(state[:, 0], "ty", [(j, i) for i, j in line])

    kept = (
        ((COLS, CH), F32),
        ((ROWS, CH), BF),
        ((ROWS, CH), BF),
        ((LAT, LON), I32),
        ((8, EDGE), I32),
        ((8, LON), I32),
        ((2 * LON + 2 * LAT, CH), F32),
        ((CH, HID), BF),
        ((3, HID, HID), BF),
        ((HID, CH), BF),
    )
    hidden = [pltpu.VMEM((TILE, HID), BF)] * 2
    held = pl.pallas_call(
        first_kernel,
        out_shape=[pltpu.VMEM(s, t) for s, t in kept],
        in_specs=[ANY] * 7,
        out_specs=[VM] * len(kept),
        scratch_shapes=[
            pltpu.VMEM((COLS + 2 * LAT + 8, CH), F32),
            pltpu.VMEM((COLS, CH), BF),
            pltpu.VMEM((LON, LAT), F32),
            pltpu.VMEM((LON, LAT), I32),
            pltpu.VMEM((LAT, LON), F32),
            pltpu.VMEM((LON, LON), F32),
            pltpu.VMEM((COLS // PGRP, PGRP), I32),
            pltpu.VMEM((PGRP, CH), F32),
            *hidden,
            pltpu.SMEM((8, LON), I32),
            pltpu.SemaphoreType.DMA((13,)),
            pltpu.SemaphoreType.DMA,
        ],
        compiler_params=pltpu.CompilerParams(vmem_limit_bytes=24 << 20),
        cost_estimate=pl.CostEstimate(flops=6_000_000_000, bytes_accessed=10 << 20, transcendentals=2 << 20),
        name="advance_pack",
    )(state.reshape(COLS, CH), courant.reshape(COLS, CH), diffusion, conv_mask, w_in, w_hidden, w_out)
    out = pl.pallas_call(
        second_kernel,
        out_shape=jax.ShapeDtypeStruct((COLS, CH), F32),
        in_specs=[VM] * 14,
        out_specs=ANY,
        scratch_shapes=[
            pltpu.VMEM((COLS, CH), F32),
            pltpu.VMEM((ROWS, CH), BF),
            pltpu.VMEM((ROWS, CH), BF),
            *hidden,
            pltpu.SMEM((8, LON), I32),
            pltpu.SemaphoreType.DMA,
            pltpu.SemaphoreType.DMA((8,)),
        ],
        compiler_params=pltpu.CompilerParams(vmem_limit_bytes=24 << 20),
        cost_estimate=pl.CostEstimate(flops=14_000_000_000, bytes_accessed=2 << 20, transcendentals=6 << 20),
        name="closure_unpack",
    )(west, east, south, north, *held)
    return out.reshape(LON, LAT, CH)


def solution(mesh):
    tile = P(("member", "tx"), "ty", None)
    flat = P(("member", "tx"), "ty")
    return jax.shard_map(
        local,
        mesh=mesh,
        in_specs=(tile, tile, flat, flat, P(), P(), P()),
        out_specs=tile,
        check_vma=False,
    )
```

time: 165 us -> 59.2 us (0.36)
  the two profiles are of different devices: /device:TPU:34 before, /device:TPU:100 now
where the time goes in v1:
time: 59.2 us; the launch traced here: 58.5 us
  Pallas kernels  37.3 us (63%)
  local copies, waits for them, and re-layouts  11.2 us (19%)
  starting transfers between devices  9.97 us (17%)
    pallas_call x1, Pallas kernels, local(): pl.pallas_call(second_kernel, out_shape=jax.ShapeDtypeStruct((COLS, CH),...  24 us
    pallas_call x1, Pallas kernels, local(): pl.pallas_call(first_kernel, out_shape=[pltpu.VMEM(s, t) for s, t in kept...  13.3 us
    unnamed x12, local copies, waits for them, and re-layouts  9.13 us
    ppermute x1, starting transfers between devices, local(): south = lax.ppermute(state[:, LAT - 1], 'ty', line)  5.04 us
    ppermute x1, starting transfers between devices, local(): east = lax.ppermute(state[0], 'tx', [(j, i) for i, j in ring])  3.01 us
    ppermute x1, starting transfers between devices, local(): north = lax.ppermute(state[:, 0], 'ty', [(j, i) for i, j in line])  1.92 us
    slice x1, local copies, waits for them, and re-layouts, local(): north = lax.ppermute(state[:, 0], 'ty', [(j, i) for i, j in line])  1.3 us
  transfers between devices with their start and end apart: 4, of which 0 were waited for; matrix products, arithmetic and copies ran while one was open for 5% of the time, Pallas kernels for 23%

profile of v1, /device:TPU:100, one launch (start us, length us, event | category | flops | bytes accessed | tf_op | source)
XLA Modules:
  0.0 58.5 jit_solution(2056661852352721065)
XLA Ops:
  0.0 0.7 %slice_bitcast_fusion = (f32[32,128]{1,0:T(8,128)S(1)}, f32[32,128]{1,0:T(8,128)S(1)}) fusion(f32[128,32,128]{2,1,0:T(8,128)} %param.7), kind=kLoop, calls=%fused_computation | loop fusion | bytes 65536 | tf_op jit(solution)/shard_map/squeeze | solution.py:278
  0.7 3.0 %collective-permute-start.1 = (f32[32,128]{1,0:T(8,128)S(1)}, f32[32,128]{1,0:T(8,128)S(1)}, u32[]{:S(2)}, u32[]{:S(2)}) collective-permute-start(f32[32,128]{1,0:T(8,128)S(1)} %get-tuple-element.27), channel_id=1, source_target_pairs={{8,0},{16,8},{24,16},{0,24},{9,1},{17,9},{25,17},{1,25},{10,2},{18... | collective-permute-start | bytes 49160 | tf_op jit(solution)/shard_map/ppermute | solution.py:278
  3.8 0.0 collective-permute-start
  3.8 1.3 %fusion = (f32[128,1,128]{2,1,0:T(1,128)S(1)}, f32[128,1,128]{2,1,0:T(1,128)S(1)}) fusion(f32[128,32,128]{2,1,0:T(8,128)} %param.7), kind=kLoop, calls=%fused_computation.2 | loop fusion | bytes 262144 | tf_op jit(solution)/shard_map/slice | solution.py:280
  5.1 5.0 %collective-permute-start.2 = (f32[128,128]{1,0:T(8,128)S(1)}, f32[128,128]{1,0:T(8,128)S(1)}, u32[]{:S(2)}, u32[]{:S(2)}) collective-permute-start(f32[128,128]{1,0:T(8,128)S(1)} %bitcast.16), channel_id=1, source_target_pairs={{0,1},{1,2},{2,3},{3,4},{4,5},{5,6},{6,7},{8,9},{9,10},{10,11},{11... | collective-permute-start | bytes 196616 | tf_op jit(solution)/shard_map/ppermute | solution.py:279
  10.1 1.9 %collective-permute-start.3 = (f32[128,128]{1,0:T(8,128)S(1)}, f32[128,128]{1,0:T(8,128)S(1)}, u32[]{:S(2)}, u32[]{:S(2)}) collective-permute-start(f32[128,128]{1,0:T(8,128)S(1)} %bitcast.15), channel_id=1, source_target_pairs={{1,0},{2,1},{3,2},{4,3},{5,4},{6,5},{7,6},{9,8},{10,9},{11,10},{12... | collective-permute-start | bytes 196616 | tf_op jit(solution)/shard_map/ppermute | solution.py:280
  12.0 0.8 %copy.10.diff_h = f32[128,32]{1,0:T(8,128)S(1)} copy(f32[128,32]{0,1:T(8,128)} %param.9) | data formatting | bytes 32768 | tf_op args[2]
  12.8 0.8 %copy.11.mask_h = s32[128,32]{1,0:T(8,128)S(1)} copy(s32[128,32]{0,1:T(8,128)} %param.10) | data formatting | bytes 32768 | tf_op args[3]
  13.7 0.0 copy-start
  13.7 1.6 %copy-done = f32[128,32,128]{2,1,0:T(8,128)S(1)} copy-done((f32[128,32,128]{2,1,0:T(8,128)S(1)}, f32[128,32,128]{2,1,0:T(8,128)}, u32[]{:S(2)}) %copy-start) | copy-done | bytes 2097176
  15.3 0.0 copy-start.1
  15.3 2.8 %copy-done.1 = bf16[3,1024,1024]{2,1,0:T(8,128)(2,1)S(1)} copy-done((bf16[3,1024,1024]{2,1,0:T(8,128)(2,1)S(1)}, bf16[3,1024,1024]{2,1,0:T(8,128)(2,1)}, u32[]{:S(2)}) %copy-start.1) | copy-done | bytes 6291480
  18.0 0.0 copy-start.2
  18.0 1.2 %copy-done.2 = bf16[128,32,128]{2,1,0:T(8,128)(2,1)S(1)} copy-done((bf16[128,32,128]{2,1,0:T(8,128)(2,1)S(1)}, bf16[128,32,128]{2,1,0:T(8,128)(2,1)}, u32[]{:S(2)}) %copy-start.2) | copy-done | bytes 1048600
  19.3 0.0 copy-start.3
  19.3 0.9 %copy-done.3 = bf16[128,1024]{1,0:T(8,128)(2,1)S(1)} copy-done((bf16[128,1024]{1,0:T(8,128)(2,1)S(1)}, bf16[128,1024]{1,0:T(8,128)(2,1)}, u32[]{:S(2)}) %copy-start.3) | copy-done | bytes 262168
  20.2 0.0 copy-start.4
  20.2 0.9 %copy-done.4 = bf16[1024,128]{1,0:T(8,128)(2,1)S(1)} copy-done((bf16[1024,128]{1,0:T(8,128)(2,1)S(1)}, bf16[1024,128]{1,0:T(8,128)(2,1)}, u32[]{:S(2)}) %copy-start.4) | copy-done | bytes 262168
  21.2 13.3 %advance_pack.1 = (f32[4096,128]{1,0:T(8,128)S(1)}, bf16[2560,128]{1,0:T(8,128)(2,1)S(1)}, bf16[2560,128]{1,0:T(8,128)(2,1)S(1)}, s32[32,128]{1,0:T(8,128)S(1)},...) custom-call(f32[4096,128]{1,0:T(8,128)S(1)} %bitcast.13, ...), custom_call_target="tpu_custom_call" | custom-call | flops 6000000000 | bytes 10485760 | tf_op jit(solution)/shard_map/advance_pack/pallas_call | solution.py:295
  34.5 0.0 collective-permute-done.1.east
  34.5 0.0 collective-permute-done.west
  34.5 0.0 collective-permute-done.2.south
  34.5 0.0 collective-permute-done.3.north
  34.5 24.0 %closure_unpack.1 = f32[4096,128]{1,0:T(8,128)} custom-call(f32[32,128]{1,0:T(8,128)S(1)} %collective-permute-done.west, f32[32,128]{1,0:T(8,128)S(1)} %collective-permute-done.1.east, f32[128,128]{1,0:T(8,128)S(1)} %collective-permute-done.2.south, f32[128,128]{1,0:T(8,128)S(1)} %collective-permute-done.3.north, f32[4096,128]{1,0:T(8,128)S(1)} %get-tuple-element.15.adv_i, ...), custom_call_target="tpu_custom_call" | custom-call | flops 14000000000 | bytes 2097152 | tf_op jit(solution)/shard_map/closure_unpack/pallas_call | solution.py:318
Async XLA Ops:
  0.7 33.7 %collective-permute-start.1 = (f32[32,128]{1,0:T(8,128)S(1)}, f32[32,128]{1,0:T(8,128)S(1)}, u32[]{:S(2)}, u32[]{:S(2)}) collective-permute-start(f32[32,128]{1,0:T(8,128)S(1)} %get-tuple-element.27), channel_id=1, source_target_pairs={{8,0},{16,8},{24,16},{0,24},{9,1},{17,9},{25,17},{1,25},{10,2},{18... | collective-permute-start | bytes 49160 | tf_op jit(solution)/shard_map/ppermute | solution.py:278
  3.8 30.7 %collective-permute-start = (f32[32,128]{1,0:T(8,128)S(1)}, f32[32,128]{1,0:T(8,128)S(1)}, u32[]{:S(2)}, u32[]{:S(2)}) collective-permute-start(f32[32,128]{1,0:T(8,128)S(1)} %get-tuple-element.28), channel_id=1, source_target_pairs={{0,8},{8,16},{16,24},{24,0},{1,9},{9,17},{17,25},{25,1},{2,10},{10... | collective-permute-start | bytes 49160 | tf_op jit(solution)/shard_map/ppermute | solution.py:277
  5.1 29.4 %collective-permute-start.2 = (f32[128,128]{1,0:T(8,128)S(1)}, f32[128,128]{1,0:T(8,128)S(1)}, u32[]{:S(2)}, u32[]{:S(2)}) collective-permute-start(f32[128,128]{1,0:T(8,128)S(1)} %bitcast.16), channel_id=1, source_target_pairs={{0,1},{1,2},{2,3},{3,4},{4,5},{5,6},{6,7},{8,9},{9,10},{10,11},{11... | collective-permute-start | bytes 196616 | tf_op jit(solution)/shard_map/ppermute | solution.py:279
  10.1 24.4 %collective-permute-start.3 = (f32[128,128]{1,0:T(8,128)S(1)}, f32[128,128]{1,0:T(8,128)S(1)}, u32[]{:S(2)}, u32[]{:S(2)}) collective-permute-start(f32[128,128]{1,0:T(8,128)S(1)} %bitcast.15), channel_id=1, source_target_pairs={{1,0},{2,1},{3,2},{4,3},{5,4},{6,5},{7,6},{9,8},{10,9},{11,10},{12... | collective-permute-start | bytes 196616 | tf_op jit(solution)/shard_map/ppermute | solution.py:280
  13.7 1.6 %copy-start = (f32[128,32,128]{2,1,0:T(8,128)S(1)}, f32[128,32,128]{2,1,0:T(8,128)}, u32[]{:S(2)}) copy-start(f32[128,32,128]{2,1,0:T(8,128)} %param.7) | copy-start | bytes 6291460
  15.3 2.8 %copy-start.1 = (bf16[3,1024,1024]{2,1,0:T(8,128)(2,1)S(1)}, bf16[3,1024,1024]{2,1,0:T(8,128)(2,1)}, u32[]{:S(2)}) copy-start(bf16[3,1024,1024]{2,1,0:T(8,128)(2,1)} %whid_h.1) | copy-start | bytes 18874372
  18.0 1.2 %copy-start.2 = (bf16[128,32,128]{2,1,0:T(8,128)(2,1)S(1)}, bf16[128,32,128]{2,1,0:T(8,128)(2,1)}, u32[]{:S(2)}) copy-start(bf16[128,32,128]{2,1,0:T(8,128)(2,1)} %param.8) | copy-start | bytes 3145732
  19.3 0.9 %copy-start.3 = (bf16[128,1024]{1,0:T(8,128)(2,1)S(1)}, bf16[128,1024]{1,0:T(8,128)(2,1)}, u32[]{:S(2)}) copy-start(bf16[128,1024]{1,0:T(8,128)(2,1)} %win_h.1) | copy-start | bytes 786436
  20.2 0.9 %copy-start.4 = (bf16[1024,128]{1,0:T(8,128)(2,1)S(1)}, bf16[1024,128]{1,0:T(8,128)(2,1)}, u32[]{:S(2)}) copy-start(bf16[1024,128]{1,0:T(8,128)(2,1)} %wout_h.1) | copy-start | bytes 786436
